TPU v7x, 128 devices: a whole 4x4x4 slice. The times are simulated.
128 devices in a mesh: row: 8 (over z, x_hi), col: 16 (over x_lo, y, core).
Axes of the slice: x: 4 (x_hi: 2, x_lo: 2; x = x_hi * 2 + x_lo), y: 4, z: 4, core: 2. Of those that a mesh axis runs over, the one named last changes fastest.
Arguments:
- features: bfloat16 [131072, 256], P(('col', 'row')), may hold values from -6 to 6
- weight: bfloat16 [256, 256], replicated, may hold values from -0.375 to 0.375
- cotangent: bfloat16 [131072, 256], P(('row', 'col')), may hold values from -6 to 6
- tile_values: bfloat16 [8, 16, 384, 128, 128], P('row', 'col')
- tile_rows: int32 [8, 16, 384], P('row', 'col'), may hold values from 0 to 127, as said below
- tile_cols: int32 [8, 16, 384], P('row', 'col'), may hold values from 0 to 63
- tile_count: int32 [8, 16], P('row', 'col'), may hold values from 96 to 384, as said below
Outputs:
- activated: bfloat16 [131072, 256], P(('row', 'col'))
- weight_grad: float32 [256, 256], replicated
- feature_grad: bfloat16 [131072, 256], P(('col', 'row'))
Inputs may be any that keep to these rules, and one draw needn't show every extreme that they name: `tile_rows`: on each device the slots name distinct (tile row, tile column) pairs. `tile_count`: some device uses all 384 slots in every draw.
All inputs are finite; a program needn't handle non-finite values.
Results may differ from a plain program's by a relative error of at most 0.025.
Values may be sent and summed in bfloat16 or wider, within the bound.
A program may use at most 192 MiB of HBM per device.

v0:
```python
import math

import jax
import jax.numpy as jnp
from jax import lax
from jax.sharding import PartitionSpec as P


def spread(values, dest, anchor, count, source, nblocks, flip):
    total = values.shape[0]
    group = math.gcd(total, 64)
    width = source.shape[-1]
    size = values.shape[1]
    nsource = source.shape[0]
    flat_source = source.reshape(nsource, size * width)
    source_ids = jnp.arange(nsource, dtype=jnp.int32)
    target_ids = jnp.arange(nblocks, dtype=jnp.int32)

    def step(index, acc):
        start = index * group
        vals = lax.dynamic_slice_in_dim(values, start, group, 0)
        target = lax.dynamic_slice_in_dim(dest, start, group, 0)
        fetch = lax.dynamic_slice_in_dim(anchor, start, group, 0)
        chooser = (fetch[:, None] == source_ids[None, :]).astype(jnp.bfloat16)
        picked = jnp.dot(chooser, flat_source, preferred_element_type=jnp.float32)
        picked = picked.astype(jnp.bfloat16).reshape(group, size, width)
        if flip:
            prod = jnp.einsum("gba,gbf->gaf", vals, picked, preferred_element_type=jnp.float32)
        else:
            prod = jnp.einsum("gab,gbf->gaf", vals, picked, preferred_element_type=jnp.float32)
        live = start + jnp.arange(group, dtype=jnp.int32) < count
        placer = ((target[:, None] == target_ids[None, :]) & live[:, None]).astype(jnp.float32)
        added = jnp.einsum("gt,gaf->taf", placer, prod, precision=lax.Precision.HIGHEST)
        return acc + added

    start_acc = jnp.zeros((nblocks, size, width), jnp.float32)
    return lax.fori_loop(0, total // group, step, start_acc)


def dense_steps(hidden, weight, cotangent):
    pre = jnp.dot(hidden, weight, preferred_element_type=jnp.float32)
    activated = jax.nn.silu(pre).astype(jnp.bfloat16)
    sig = jax.nn.sigmoid(pre)
    delta = (cotangent.astype(jnp.float32) * sig * (1.0 + pre * (1.0 - sig))).astype(jnp.bfloat16)
    return (activated, delta)


def per_device(features, weight, cotangent, tile_values, tile_rows, tile_cols, tile_count):
    values = tile_values[0, 0]
    rows_idx = tile_rows[0, 0]
    cols_idx = tile_cols[0, 0]
    count = tile_count[0, 0]
    size = values.shape[1]
    width = features.shape[1]
    node_dev = features.shape[0]
    n_row = lax.axis_size("row")
    n_col = lax.axis_size("col")
    row_blocks = node_dev * n_col // size
    col_blocks = node_dev * n_row // size
    panel = lax.all_gather(features, "row", axis=0, tiled=True).reshape(col_blocks, size, width)
    part = spread(values, rows_idx, cols_idx, count, panel, row_blocks, False).reshape(
        row_blocks * size, width
    )
    part = part.astype(jnp.bfloat16)
    hidden = (
        lax.psum_scatter(part, "col", scatter_dimension=0, tiled=True)
        .astype(jnp.float32)
        .astype(jnp.bfloat16)
    )
    activated, delta = dense_steps(hidden, weight, cotangent)
    back = jnp.dot(delta, weight.T, preferred_element_type=jnp.float32).astype(jnp.bfloat16)
    back_block = lax.all_gather(back, "col", axis=0, tiled=True)
    grad_terms = jnp.einsum("nf,ng->fg", hidden, delta, preferred_element_type=jnp.float32)
    total_nodes = node_dev * n_row * n_col
    weight_grad = lax.psum(grad_terms, ("row", "col")) / jnp.sqrt(jnp.float32(total_nodes))
    source = back_block.reshape(row_blocks, size, width)
    tpart = spread(values, cols_idx, rows_idx, count, source, col_blocks, True).reshape(
        col_blocks * size, width
    )
    tpart = tpart.astype(jnp.bfloat16)
    feature_grad = (
        lax.psum_scatter(tpart, "row", scatter_dimension=0, tiled=True)
        .astype(jnp.float32)
        .astype(jnp.bfloat16)
    )
    return (activated, weight_grad, feature_grad)


def solution(mesh):
    return jax.shard_map(
        per_device,
        mesh=mesh,
        in_specs=(
            P(("col", "row"), None),
            P(),
            P(("row", "col"), None),
            P("row", "col", None, None, None),
            P("row", "col", None),
            P("row", "col", None),
            P("row", "col"),
        ),
        out_specs=(P(("row", "col"), None), P(), P(("col", "row"), None)),
        check_vma=False,
    )
```

profile of v0, /device:TPU:0, one launch (start us, length us, event | category | flops | bytes accessed | tf_op | source)
XLA Modules:
  0.0 732.8 jit_solution(3134430029858656934)
XLA Ops:
  9.4 75.1 %all-gather.3.cloned.1.call-done = bf16[8192,256]{1,0:T(8,128)(2,1)} async-done(((bf16[1024,256]{1,0:T(8,128)(2,1)}), bf16[8192,256]{1,0:T(8,128)(2,1)}) %all-gather.3.cloned.1.call-update) | async-done | bytes 4194320 | tf_op jit(solution)/shard_map/all_gather | solution.py:60
  84.4 7.4 %reshape_reshape.6 = bf16[64,32768]{1,0:T(8,128)(2,1)} reshape(bf16[8192,256]{1,0:T(8,128)(2,1)} %all-gather.3.cloned.1.call-done) | data formatting | bytes 8388608 | tf_op jit(solution)/shard_map/reshape;reshape | solution.py:15
  91.8 196.9 %while.28 = (s32[]{:T(128)}, f32[128,128,256]{2,0,1:T(8,128)}, s32[384]{0:T(512)S(1)}, s32[]{:T(128)}, bf16[384,128,128]{2,1,0:T(8,128)(2,1)}, /*index=5*/s32[38...) while((s32[]{:T(128)}, f32[128,128,256]{2,0,1:T(8,128)}, ...), condition=%wide.region_1.0_spmd.clone, body=%wide.region_0.0_spmd.clone.sunk | while | flops 4037038080 | bytes 73402168 | solution.py:37
  103.3 19.3 %select_add_fusion.4 = f32[128,128,256]{2,0,1:T(8,128)} fusion(f32[128,128,256]{2,0,1:T(8,128)} %get-tuple-element.497, f32[64,128,256]{2,1,0:T(8,128)} %fusion.59, pred[]{:T(512)S(6)} %compare.6, s32[64]{0:T(128)S(1)} %dynamic_slice.60, pred[64]{0:T(512)(128)(4,1)S(1)} %add_compare_fusion.4), kind=kOutput, calls=%fused_computation.5.clone.1 | convolution fusion | flops 3229630464 | bytes 41943360 | tf_op jit(solution)/shard_map/while/body/eval_jaxpr/gt,gaf->taf/dot_general | solution.py:33
  134.1 21.7 %select_add_fusion.4 = f32[128,128,256]{2,0,1:T(8,128)} fusion(f32[128,128,256]{2,0,1:T(8,128)} %get-tuple-element.497, f32[64,128,256]{2,1,0:T(8,128)} %fusion.59, pred[]{:T(512)S(6)} %compare.6, s32[64]{0:T(128)S(1)} %dynamic_slice.60, pred[64]{0:T(512)(128)(4,1)S(1)} %add_compare_fusion.4), kind=kOutput, calls=%fused_computation.5.clone.1 | convolution fusion | flops 3229630464 | bytes 41943360 | tf_op jit(solution)/shard_map/while/body/eval_jaxpr/gt,gaf->taf/dot_general | solution.py:33
  167.3 21.8 %select_add_fusion.4 = f32[128,128,256]{2,0,1:T(8,128)} fusion(f32[128,128,256]{2,0,1:T(8,128)} %get-tuple-element.497, f32[64,128,256]{2,1,0:T(8,128)} %fusion.59, pred[]{:T(512)S(6)} %compare.6, s32[64]{0:T(128)S(1)} %dynamic_slice.60, pred[64]{0:T(512)(128)(4,1)S(1)} %add_compare_fusion.4), kind=kOutput, calls=%fused_computation.5.clone.1 | convolution fusion | flops 3229630464 | bytes 41943360 | tf_op jit(solution)/shard_map/while/body/eval_jaxpr/gt,gaf->taf/dot_general | solution.py:33
  200.6 21.7 %select_add_fusion.4 = f32[128,128,256]{2,0,1:T(8,128)} fusion(f32[128,128,256]{2,0,1:T(8,128)} %get-tuple-element.497, f32[64,128,256]{2,1,0:T(8,128)} %fusion.59, pred[]{:T(512)S(6)} %compare.6, s32[64]{0:T(128)S(1)} %dynamic_slice.60, pred[64]{0:T(512)(128)(4,1)S(1)} %add_compare_fusion.4), kind=kOutput, calls=%fused_computation.5.clone.1 | convolution fusion | flops 3229630464 | bytes 41943360 | tf_op jit(solution)/shard_map/while/body/eval_jaxpr/gt,gaf->taf/dot_general | solution.py:33
  233.8 21.8 %select_add_fusion.4 = f32[128,128,256]{2,0,1:T(8,128)} fusion(f32[128,128,256]{2,0,1:T(8,128)} %get-tuple-element.497, f32[64,128,256]{2,1,0:T(8,128)} %fusion.59, pred[]{:T(512)S(6)} %compare.6, s32[64]{0:T(128)S(1)} %dynamic_slice.60, pred[64]{0:T(512)(128)(4,1)S(1)} %add_compare_fusion.4), kind=kOutput, calls=%fused_computation.5.clone.1 | convolution fusion | flops 3229630464 | bytes 41943360 | tf_op jit(solution)/shard_map/while/body/eval_jaxpr/gt,gaf->taf/dot_general | solution.py:33
  267.0 21.7 %select_add_fusion.4 = f32[128,128,256]{2,0,1:T(8,128)} fusion(f32[128,128,256]{2,0,1:T(8,128)} %get-tuple-element.497, f32[64,128,256]{2,1,0:T(8,128)} %fusion.59, pred[]{:T(512)S(6)} %compare.6, s32[64]{0:T(128)S(1)} %dynamic_slice.60, pred[64]{0:T(512)(128)(4,1)S(1)} %add_compare_fusion.4), kind=kOutput, calls=%fused_computation.5.clone.1 | convolution fusion | flops 3229630464 | bytes 41943360 | tf_op jit(solution)/shard_map/while/body/eval_jaxpr/gt,gaf->taf/dot_general | solution.py:33
  288.8 17.0 %copy.24 = bf16[128,128,256]{2,1,0:T(8,128)(2,1)} copy(f32[128,128,256]{2,0,1:T(8,128)} %get-tuple-element.311) | data formatting | bytes 25165824 | tf_op jit(solution)/shard_map/while | solution.py:37
  305.8 72.6 %reduce-scatter.3.cloned.1.call-done = bf16[1024,256]{1,0:T(8,128)(2,1)} async-done(((bf16[16384,256]{1,0:T(8,128)(2,1)}), bf16[1024,256]{1,0:T(8,128)(2,1)}) %reduce-scatter.3.cloned.1.call-update) | async-done | bytes 524304 | tf_op jit(solution)/shard_map/reduce_scatter | solution.py:66
  383.4 49.4 %all-gather.5.cloned.1.call-done = bf16[16384,256]{1,0:T(8,128)(2,1)} async-done(((bf16[1024,256]{1,0:T(8,128)(2,1)}), bf16[16384,256]{1,0:T(8,128)(2,1)}) %all-gather.5.cloned.1.call-update) | async-done | bytes 8388624 | tf_op jit(solution)/shard_map/all_gather | solution.py:72
  432.8 13.5 %reshape_reshape.7 = bf16[128,32768]{1,0:T(8,128)(2,1)} reshape(bf16[16384,256]{1,0:T(8,128)(2,1)} %all-gather.5.cloned.1.call-done) | data formatting | bytes 16777216 | tf_op jit(solution)/shard_map/reshape;reshape | solution.py:15
  446.3 185.6 %while.29 = (s32[]{:T(128)}, f32[64,128,256]{2,0,1:T(8,128)}, s32[384]{0:T(512)S(1)}, s32[]{:T(128)}, bf16[384,128,128]{2,1,0:T(8,128)(2,1)}, /*index=5*/s32[384...) while((s32[]{:T(128)}, f32[64,128,256]{2,0,1:T(8,128)}, ...), condition=%wide.region_5.6_spmd.clone, body=%wide.region_4.5_spmd.clone.sunk | while | flops 2690662400 | bytes 60819256 | solution.py:37
  459.1 16.2 %select_add_fusion.5 = f32[64,128,256]{2,0,1:T(8,128)} fusion(f32[64,128,256]{2,0,1:T(8,128)} %get-tuple-element.530, pred[]{:T(512)S(6)} %compare.7, f32[64,128,256]{2,1,0:T(8,128)} %fusion.65, s32[64]{0:T(128)S(1)} %dynamic_slice.63, pred[64]{0:T(512)(128)(4,1)S(1)} %add_compare_fusion.5), kind=kOutput, calls=%fused_computation.21.clone.1 | convolution fusion | flops 1614815232 | bytes 25166144 | tf_op jit(solution)/shard_map/while/body/eval_jaxpr/gt,gaf->taf/dot_general | solution.py:33
  488.0 18.6 %select_add_fusion.5 = f32[64,128,256]{2,0,1:T(8,128)} fusion(f32[64,128,256]{2,0,1:T(8,128)} %get-tuple-element.530, pred[]{:T(512)S(6)} %compare.7, f32[64,128,256]{2,1,0:T(8,128)} %fusion.65, s32[64]{0:T(128)S(1)} %dynamic_slice.63, pred[64]{0:T(512)(128)(4,1)S(1)} %add_compare_fusion.5), kind=kOutput, calls=%fused_computation.21.clone.1 | convolution fusion | flops 1614815232 | bytes 25166144 | tf_op jit(solution)/shard_map/while/body/eval_jaxpr/gt,gaf->taf/dot_general | solution.py:33
  519.4 18.6 %select_add_fusion.5 = f32[64,128,256]{2,0,1:T(8,128)} fusion(f32[64,128,256]{2,0,1:T(8,128)} %get-tuple-element.530, pred[]{:T(512)S(6)} %compare.7, f32[64,128,256]{2,1,0:T(8,128)} %fusion.65, s32[64]{0:T(128)S(1)} %dynamic_slice.63, pred[64]{0:T(512)(128)(4,1)S(1)} %add_compare_fusion.5), kind=kOutput, calls=%fused_computation.21.clone.1 | convolution fusion | flops 1614815232 | bytes 25166144 | tf_op jit(solution)/shard_map/while/body/eval_jaxpr/gt,gaf->taf/dot_general | solution.py:33
  543.8 6.2 fusion.65
  550.7 18.6 %select_add_fusion.5 = f32[64,128,256]{2,0,1:T(8,128)} fusion(f32[64,128,256]{2,0,1:T(8,128)} %get-tuple-element.530, pred[]{:T(512)S(6)} %compare.7, f32[64,128,256]{2,1,0:T(8,128)} %fusion.65, s32[64]{0:T(128)S(1)} %dynamic_slice.63, pred[64]{0:T(512)(128)(4,1)S(1)} %add_compare_fusion.5), kind=kOutput, calls=%fused_computation.21.clone.1 | convolution fusion | flops 1614815232 | bytes 25166144 | tf_op jit(solution)/shard_map/while/body/eval_jaxpr/gt,gaf->taf/dot_general | solution.py:33
  575.2 6.2 fusion.65
  582.1 18.6 %select_add_fusion.5 = f32[64,128,256]{2,0,1:T(8,128)} fusion(f32[64,128,256]{2,0,1:T(8,128)} %get-tuple-element.530, pred[]{:T(512)S(6)} %compare.7, f32[64,128,256]{2,1,0:T(8,128)} %fusion.65, s32[64]{0:T(128)S(1)} %dynamic_slice.63, pred[64]{0:T(512)(128)(4,1)S(1)} %add_compare_fusion.5), kind=kOutput, calls=%fused_computation.21.clone.1 | convolution fusion | flops 1614815232 | bytes 25166144 | tf_op jit(solution)/shard_map/while/body/eval_jaxpr/gt,gaf->taf/dot_general | solution.py:33
  606.5 6.2 fusion.65
  613.4 18.6 %select_add_fusion.5 = f32[64,128,256]{2,0,1:T(8,128)} fusion(f32[64,128,256]{2,0,1:T(8,128)} %get-tuple-element.530, pred[]{:T(512)S(6)} %compare.7, f32[64,128,256]{2,1,0:T(8,128)} %fusion.65, s32[64]{0:T(128)S(1)} %dynamic_slice.63, pred[64]{0:T(512)(128)(4,1)S(1)} %add_compare_fusion.5), kind=kOutput, calls=%fused_computation.21.clone.1 | convolution fusion | flops 1614815232 | bytes 25166144 | tf_op jit(solution)/shard_map/while/body/eval_jaxpr/gt,gaf->taf/dot_general | solution.py:33
  642.1 84.1 %reduce-scatter.5.cloned.1.call-done = bf16[1024,256]{1,0:T(8,128)(2,1)} async-done(((bf16[8192,256]{1,0:T(8,128)(2,1)}), bf16[1024,256]{1,0:T(8,128)(2,1)}) %reduce-scatter.5.cloned.1.call-update) | async-done | bytes 524304 | tf_op jit(solution)/shard_map/reduce_scatter | solution.py:82
  (98 shorter events, 144.0 us)
Async XLA Ops:
  7.2 371.3 %copy-start = (bf16[256,256]{1,0:T(8,128)(2,1)S(1)}, bf16[256,256]{1,0:T(8,128)(2,1)}, u32[]{:S(2)}) copy-start(bf16[256,256]{1,0:T(8,128)(2,1)} %param.12) | copy-start | bytes 393220
  7.2 77.2 %all-gather.3.cloned.1.call-start = ((), (), s32[]{:S(2)}) async-start(), calls=%async_computation.2 | async-start | bytes 4718592 | tf_op jit(solution)/shard_map/all_gather | solution.py:60
  7.9 370.5 %reduce-scatter.3.cloned.1.call-start = ((), (), s32[]{:S(2)}) async-start(), calls=%async_computation.3 | async-start | bytes 8912896 | tf_op jit(solution)/shard_map/reduce_scatter | solution.py:66
  305.8 72.7 %copy-start.3 = (bf16[1024,256]{1,0:T(8,128)(2,1)S(1)}, bf16[1024,256]{1,0:T(8,128)(2,1)}, u32[]{:S(2)}) copy-start(bf16[1024,256]{1,0:T(8,128)(2,1)} %param.13) | copy-start | bytes 1572868
  305.8 127.0 %all-gather.5.cloned.1.call-start = ((), (), s32[]{:S(2)}) async-start(), calls=%async_computation.5 | async-start | bytes 8912896 | tf_op jit(solution)/shard_map/all_gather | solution.py:72
  378.5 3.8 copy-start.2
  382.2 258.2 %all-reduce.2.cloned.1.call-start = ((), (), s32[]{:S(2)}) async-start(), calls=%async_computation.4 | async-start | bytes 524288 | tf_op jit(solution)/shard_map/psum | solution.py:75
  383.3 342.9 %reduce-scatter.5.cloned.1.call-start = ((), (), s32[]{:S(2)}) async-start(), calls=%async_computation.6 | async-start | bytes 4718592 | tf_op jit(solution)/shard_map/reduce_scatter | solution.py:82
  631.9 94.3 %copy-start.1 = (bf16[256,256]{1,0:T(8,128)(2,1)S(1)}, bf16[256,256]{1,0:T(8,128)(2,1)}, u32[]{:S(2)}) copy-start(bf16[256,256]{1,0:T(8,128)(2,1)} %param.12) | copy-start | bytes 393220
Sparse Core Ops, SparseCore 0:
  10.4 74.0 all-gather.2
  305.9 72.5 reduce-scatter.2
  382.3 50.4 all-gather.4
  438.0 142.9 all-reduce.1
  640.5 85.6 reduce-scatter.4
where the time goes:
time: 734 us; the launch traced here: 733 us
  matrix products  364 us (50%)
  waiting for transfers between devices  282 us (38%)
  local copies, waits for them, and re-layouts  57.2 us (8%)
  other arithmetic  14.9 us (2%)
  between operations  13.8 us (2%)
    dot_general x12, matrix products, step(): jnp.einsum('gt,gaf->taf', placer, prod, precision=lax.Precision.HIGHEST)  237 us
    reduce_scatter x1, waiting for transfers between devices, per_device(): lax.psum_scatter(tpart, 'row', scatter_dimension=0, tiled=True)  84.1 us
    all_gather x1, waiting for transfers between devices, per_device(): lax.all_gather(features, 'row', axis=0, tiled=True)  75.1 us
    reduce_scatter x1, waiting for transfers between devices, per_device(): lax.psum_scatter(part, 'col', scatter_dimension=0, tiled=True)  72.6 us
    all_gather x1, waiting for transfers between devices, per_device(): back_block = lax.all_gather(back, 'col', axis=0, tiled=True)  49.4 us
    dot_general x12, matrix products, step(): picked = jnp.dot(chooser, flat_source, preferred_element_type=jnp.float32)  49 us
    dot_general x6, matrix products, step(): jnp.einsum('gba,gbf->gaf', vals, picked, preferred_element_type=jnp.float32)  36.9 us
    dot_general x6, matrix products, step(): jnp.einsum('gab,gbf->gaf', vals, picked, preferred_element_type=jnp.float32)  36.6 us
  transfers between devices with their start and end apart: 5, of which 4 were waited for; matrix products, arithmetic and copies ran while one was open for 29% of the time, Pallas kernels for 0%

commit v1 on v0

v1 whole, which is shorter than its diff:
```python
import functools

import jax
import jax.numpy as jnp
from jax import lax
from jax.experimental import pallas as pl
from jax.experimental.pallas import tpu as pltpu
from jax.sharding import PartitionSpec as P

BF16 = jnp.bfloat16
F32 = jnp.float32
UNROLL = 24
SIDE = 128


def place():
    r = lax.axis_index("row")
    c = lax.axis_index("col")
    return r // 2, r % 2, c // 8, (c // 2) % 4, c % 2


def row_device(z, xh):
    return (z * 2 + xh, lax.axis_index("col"))


def col_device(xl, y, k):
    return (lax.axis_index("row"), xl * 8 + y * 2 + k)


def greet(peers):
    barrier = pltpu.get_barrier_semaphore()
    for peer in peers:
        pl.semaphore_signal(barrier, inc=1, device_id=peer, device_id_type=pl.DeviceIdType.MESH)
    pl.semaphore_wait(barrier, len(peers))


class Mover:
    def __init__(self, send_sem, recv_sem, local_sem):
        self.send_sem, self.recv_sem, self.local_sem = send_sem, recv_sem, local_sem
        self.started = 0
        self.kept = 0
        self.pending = []

    def remote(self, src, dst, device):
        at = self.started
        self.started += 1
        copy = pltpu.make_async_remote_copy(
            src_ref=src,
            dst_ref=dst,
            send_sem=self.send_sem.at[at],
            recv_sem=self.recv_sem.at[at],
            device_id=device,
            device_id_type=pl.DeviceIdType.MESH,
        )
        copy.start()
        self.pending.append(copy)
        return copy

    def local(self, src, dst):
        copy = pltpu.make_async_copy(src, dst, self.local_sem.at[self.kept])
        copy.start()
        self.kept += 1
        return copy

    def drain(self):
        for copy in self.take():
            copy.wait_send()

    def take(self):
        copies, self.pending = self.pending, []
        return copies


def add_blocks(dst, terms, blocks):
    def body(i, carry):
        total = terms[0][i].astype(F32)
        for term in terms[1:]:
            total = total + term[i].astype(F32)
        dst[i] = total.astype(dst.dtype)
        return carry

    lax.fori_loop(0, blocks, body, 0)


def split(blocks):
    first = blocks // 4
    rest = blocks - first
    return {
        "A": (0, first),
        "A0": (0, first // 2),
        "A1": (first // 2, first // 2),
        "B": (first, rest),
        "B0": (first, rest // 2),
        "B1": (first + rest // 2, rest // 2),
    }


class Links:
    def __init__(self, ring, pair, p, q, slot, blocks):
        self.ring, self.pair, self.p, self.q, self.slot, self.blocks = ring, pair, p, q, slot, blocks

    def piece(self, d, side):
        return self.slot((self.p + d) % 4, self.q if side == 0 else 1 - self.q)

    def part(self, ref, d, side, name=None):
        start, size = split(self.blocks)[name] if name else (0, self.blocks)
        return ref.at[pl.ds(self.piece(d, side) * self.blocks + start, size)]


def gather_steps(mv, links, out, arrived):
    plus, minus = links.ring
    pair = links.pair
    reg = functools.partial(links.part, out)

    def go(d, side, name, device):
        return mv.remote(reg(d, side, name), reg(d, side, name), device)

    pair_b = go(0, 0, "B", pair)
    a_plus = go(0, 0, "A", plus)
    a_minus = go(0, 0, "A", minus)
    b_plus = go(0, 0, "B", plus)
    b_minus = go(0, 0, "B", minus)
    pair_a = [go(0, 0, "A", pair)]
    yield
    a_plus.wait_recv()
    ra_plus = go(3, 0, "A0", plus)
    pair_a.append(go(3, 0, "A", pair))
    a_minus.wait_recv()
    ra_minus = go(1, 0, "A1", minus)
    pair_a.append(go(1, 0, "A", pair))
    arrived(reg(3, 0, "A"))
    arrived(reg(1, 0, "A"))
    yield
    pair_b.wait_recv()
    pb_plus = go(0, 1, "B", plus)
    pb_minus = go(0, 1, "B", minus)
    arrived(reg(0, 1, "B"))
    yield
    b_plus.wait_recv()
    rb_plus = go(3, 0, "B0", plus)
    b_minus.wait_recv()
    rb_minus = go(1, 0, "B1", minus)
    arrived(reg(3, 0, "B"))
    arrived(reg(1, 0, "B"))
    yield
    ra_plus.wait_recv()
    pair_a.append(go(2, 0, "A0", pair))
    ra_minus.wait_recv()
    pair_a.append(go(2, 0, "A1", pair))
    arrived(reg(2, 0, "A"))
    yield
    pb_plus.wait_recv()
    rpb_plus = go(3, 1, "B0", plus)
    pb_minus.wait_recv()
    rpb_minus = go(1, 1, "B1", minus)
    arrived(reg(3, 1, "B"))
    arrived(reg(1, 1, "B"))
    yield
    rb_plus.wait_recv()
    rb_minus.wait_recv()
    arrived(reg(2, 0, "B"))
    for d, copy in zip((0, 3, 1), pair_a):
        yield
        copy.wait_recv()
        arrived(reg(d, 1, "A"))
    yield
    pair_a[3].wait_recv()
    pair_a[4].wait_recv()
    arrived(reg(2, 1, "A"))
    yield
    rpb_plus.wait_recv()
    rpb_minus.wait_recv()
    arrived(reg(2, 1, "B"))


def scatter_scratch(blocks):
    parts = split(blocks)
    first, rest = parts["A"][1], parts["B"][1]
    return [
        pltpu.VMEM((4, first, SIDE, SIDE), BF16),
        pltpu.VMEM((2, 2, rest // 2, SIDE, SIDE), BF16),
        pltpu.VMEM((2, 2, rest, SIDE, SIDE), BF16),
        pltpu.VMEM((2, first // 2, SIDE, SIDE), BF16),
        pltpu.VMEM((2, first, SIDE, SIDE), BF16),
        pltpu.VMEM((rest, SIDE, SIDE), BF16),
    ]


ORDER = ((2, 1), (2, 0), (1, 1), (3, 1), (1, 0), (3, 0), (0, 1), (0, 0))


def scatter_steps(mv, links, held, bufs, out, ready):
    parts = split(links.blocks)
    plus, minus = links.ring
    pair = links.pair
    ra, rb1, rb2, ra1, ra2, rp = bufs
    nb, na = parts["B"][1], parts["A"][1]
    reg = functools.partial(links.part, held)
    b_half = lambda ref, h: ref.at[pl.ds(h * (nb // 2), nb // 2)]
    a_half = lambda ref, h: ref.at[pl.ds(h * (na // 2), na // 2)]
    got_b1, got_b2, got_a, got_a2 = {}, {}, {}, {}
    for d, side in ORDER:
        yield
        ready(d, side)
        if d == 2:
            got_b1[0, side] = mv.remote(reg(2, side, "B0"), rb1.at[0, side], plus)
            got_b1[1, side] = mv.remote(reg(2, side, "B1"), rb1.at[1, side], minus)
        elif d == 1:
            got_b2[0, side, 1] = mv.remote(reg(1, side, "B1"), b_half(rb2.at[0, side], 1), plus)
        elif d == 3:
            got_b2[1, side, 0] = mv.remote(reg(3, side, "B0"), b_half(rb2.at[1, side], 0), minus)
        if side == 1:
            got_a[d] = mv.remote(reg(d, 1, "A"), ra.at[d], pair)
    for side in (1, 0):
        yield
        got_b1[0, side].wait_recv()
        add_blocks(reg(1, side, "B0"), [reg(1, side, "B0"), rb1.at[0, side]], nb // 2)
        got_b2[0, side, 0] = mv.remote(reg(1, side, "B0"), b_half(rb2.at[0, side], 0), plus)
        got_b1[1, side].wait_recv()
        add_blocks(reg(3, side, "B1"), [reg(3, side, "B1"), rb1.at[1, side]], nb // 2)
        got_b2[1, side, 1] = mv.remote(reg(3, side, "B1"), b_half(rb2.at[1, side], 1), minus)
    yield
    got_a[2].wait_recv()
    add_blocks(reg(2, 0, "A"), [reg(2, 0, "A"), ra.at[2]], na)
    got_a1 = [
        mv.remote(reg(2, 0, "A0"), ra1.at[0], plus),
        mv.remote(reg(2, 0, "A1"), ra1.at[1], minus),
    ]
    yield
    got_a[1].wait_recv()
    add_blocks(reg(1, 0, "A"), [reg(1, 0, "A"), ra.at[1]], na)
    got_a2[0, 1] = mv.remote(reg(1, 0, "A1"), a_half(ra2.at[0], 1), plus)
    got_a[3].wait_recv()
    add_blocks(reg(3, 0, "A"), [reg(3, 0, "A"), ra.at[3]], na)
    got_a2[1, 0] = mv.remote(reg(3, 0, "A0"), a_half(ra2.at[1], 0), minus)
    yield
    for way in (0, 1):
        for h in (0, 1):
            got_b2[way, 1, h].wait_recv()
    add_blocks(reg(0, 1, "B"), [reg(0, 1, "B"), rb2.at[0, 1], rb2.at[1, 1]], nb)
    got_p = mv.remote(reg(0, 1, "B"), rp, pair)
    yield
    got_a1[0].wait_recv()
    add_blocks(reg(1, 0, "A0"), [reg(1, 0, "A0"), ra1.at[0]], na // 2)
    got_a2[0, 0] = mv.remote(reg(1, 0, "A0"), a_half(ra2.at[0], 0), plus)
    got_a1[1].wait_recv()
    add_blocks(reg(3, 0, "A1"), [reg(3, 0, "A1"), ra1.at[1]], na // 2)
    got_a2[1, 1] = mv.remote(reg(3, 0, "A1"), a_half(ra2.at[1], 1), minus)
    yield
    for way in (0, 1):
        for h in (0, 1):
            got_b2[way, 0, h].wait_recv()
    got_p.wait_recv()
    add_blocks(out.at[pl.ds(na, nb)], [reg(0, 0, "B"), rb2.at[0, 0], rb2.at[1, 0], rp], nb)
    yield
    got_a[0].wait_recv()
    for way in (0, 1):
        for h in (0, 1):
            got_a2[way, h].wait_recv()
    add_blocks(out.at[pl.ds(0, na)], [reg(0, 0, "A"), ra.at[0], ra2.at[0], ra2.at[1]], na)


def spread_steps(plan, base, flip, tiles, source, staged, out, blocks, cuts):
    total = tiles.shape[0]
    perm, anchor, fresh, last, has = (functools.partial(lambda row, i: plan[row, i], base + j) for j in range(5))

    def body(i, acc):
        first = i * UNROLL
        prods = []
        for u in range(UNROLL):
            tile = tiles[perm(first + u)]
            other = source[anchor(first + u)]
            left, right = (other, tile) if flip else (tile, other)
            prods.append(jnp.dot(left, right, preferred_element_type=F32))
        for u in range(UNROLL):
            begins = jnp.full((SIDE, SIDE), fresh(first + u), jnp.int32) != 0
            acc = jnp.where(begins, 0.0, acc) + prods[u]
            staged[first + u] = acc.astype(BF16)
        return acc

    steps = total // UNROLL
    acc = jnp.zeros((SIDE, SIDE), F32)
    for cut in range(cuts):
        acc = lax.fori_loop(cut * steps // cuts, (cut + 1) * steps // cuts, body, acc)
        if cut < cuts - 1:
            yield

    group = 8

    def put(i, carry):
        for v in range(group):
            r = i * group + v
            filled = jnp.full((SIDE, SIDE), has(r), jnp.int32) != 0
            out[r] = jnp.where(filled, staged[last(r)].astype(F32), 0.0).astype(BF16)
        return carry

    lax.fori_loop(0, blocks // group, put, 0)


def reduce_steps(mv, gt, wr1, wr2, wg_ref, row_peers, col_peers, nodes):
    r0 = lax.axis_index("row")
    c0 = lax.axis_index("col")
    n_row, n_col = len(row_peers) + 1, len(col_peers) + 1
    depth = gt.shape[0] // n_col

    def strip(c):
        return pl.ds(pl.multiple_of(c * depth, depth), depth)

    first = [
        mv.remote(gt.at[strip((c0 + j) % n_col)], wr1.at[j], col_peers[j - 1])
        for j in range(1, n_col)
    ]
    yield
    for copy in first:
        copy.wait_recv()
    total = gt[strip(c0), :]
    for j in range(1, n_col):
        total = total + wr1[j]
    wr2[r0] = total
    second = [mv.remote(wr2.at[r0], wr2.at[r0], peer) for peer in row_peers]
    yield
    for copy in second:
        copy.wait_recv()
    total = wr2[0]
    for j in range(1, n_row):
        total = total + wr2[j]
    wg_ref[strip(c0), :] = total / jnp.sqrt(F32(nodes))
    third = [mv.remote(wg_ref.at[strip(c0)], wg_ref.at[strip(c0)], peer) for peer in col_peers]
    yield
    for copy in third:
        copy.wait_recv()


def advance(steps, count=None):
    taken = 0
    while count is None or taken < count:
        try:
            next(steps)
        except StopIteration:
            return False
        taken += 1
    return True


def braid(*streams):
    left = list(streams)
    while left:
        left = [s for s in left if advance(s, 1)]


def layer_kernel(
    nodes, plan, x_ref, w_ref, cot_ref, tiles_ref, act_ref, wg_ref, fg_ref,
    tiles, staged, panel0, panel1, part0, part1, met0, met1, back0, back1,
    hid0, hid1, delta, cot, fgt0, fgt1, gt, wr1, wr2, *rest
):
    f_bufs = (rest[0:6], rest[6:12])
    b_bufs = (rest[12:18], rest[18:24])
    mv = Mover(*rest[24:27])
    panel, part, met, back = (panel0, panel1), (part0, part1), (met0, met1), (back0, back1)
    hid, fgt = (hid0, hid1), (fgt0, fgt1)
    z, xh, xl, y, k = place()
    r0, c0 = lax.axis_index("row"), lax.axis_index("col")
    rows = cot.shape[0]
    blocks = rows // SIDE
    n_row, n_col = lax.axis_size("row"), lax.axis_size("col")

    row_slot = lambda p, q: p * 2 + q
    col_slot = lambda p, q: (q * 4 + p) * 2 + k
    row_links = Links(
        (row_device((z + 1) % 4, xh), row_device((z + 3) % 4, xh)),
        row_device(z, 1 - xh), z, xh, row_slot, blocks)
    col_links = Links(
        (col_device(xl, (y + 1) % 4, k), col_device(xl, (y + 3) % 4, k)),
        col_device(1 - xl, y, k), y, xl, col_slot, blocks)
    twin = col_device(xl, y, 1 - k)

    loads = [
        mv.local(x_ref.at[:, :, pl.ds(h * SIDE, SIDE)], row_links.part(panel[h], 0, 0)) for h in (0, 1)
    ]
    load_tiles = mv.local(tiles_ref, tiles)
    load_cot = mv.local(cot_ref, cot)
    row_peers = [((r0 + j) % n_row, c0) for j in range(1, n_row)]
    col_peers = [(r0, (c0 + j) % n_col) for j in range(1, n_col)]
    greet(row_peers + col_peers)

    gathers = [gather_steps(mv, row_links, panel[h], lambda ref: None) for h in (0, 1)]
    loads[0].wait()
    advance(gathers[0], 4)
    loads[1].wait()
    while advance(gathers[0], 1):
        advance(gathers[1], 1)
    load_tiles.wait()

    def twin_steps(h):
        crossing = {}
        for d, side in ORDER:
            piece = (y + d) % 4 + 4 * (xl if side == 0 else 1 - xl)
            from_part = part[h].at[pl.ds((piece * 2 + 1 - k) * blocks, blocks)]
            to_met = met[h].at[pl.ds(piece * blocks, blocks)]
            crossing[d, side] = (mv.remote(from_part, to_met, twin), to_met)

        def ready(d, side):
            copy, land = crossing[d, side]
            copy.wait_recv()
            ref = col_links.part(part[h], d, side)
            add_blocks(ref, [ref, land], blocks)

        yield from scatter_steps(mv, col_links, part[h], f_bufs[h], hid[h], ready)

    cuts = 8
    spread = [
        spread_steps(plan, 0, False, tiles, panel[h], staged, part[h], part[h].shape[0], cuts)
        for h in (0, 1)
    ]
    while advance(spread[0], 1):
        advance(gathers[1], 1)
    scatters = [twin_steps(h) for h in (0, 1)]
    advance(scatters[0], 4)
    while advance(gathers[1], 1):
        advance(scatters[0], 1)
    while advance(spread[1], 1):
        advance(scatters[0], 1)
    forward_sends = mv.take()
    advance(scatters[1], 8)
    braid(scatters[0], scatters[1])

    load_cot.wait()
    weight = w_ref[...]
    mine = col_links.piece(0, 0) * blocks

    def dense(i, carry):
        at = pl.ds(pl.multiple_of(i * SIDE, SIDE), SIDE)
        hidden = jnp.concatenate([hid0[i], hid1[i]], axis=1)
        pre = jnp.dot(hidden, weight, preferred_element_type=F32)
        sig = 1.0 / (1.0 + jnp.exp(-pre))
        act_ref[at, :] = (pre * sig).astype(BF16)
        d = (cot[at, :].astype(F32) * sig * (1.0 + pre * (1.0 - sig))).astype(BF16)
        delta[at, :] = d
        turned = lax.dot_general(
            weight, d, (((1,), (1,)), ((), ())), preferred_element_type=F32
        ).astype(BF16)
        for h in (0, 1):
            back[h][mine + i] = turned[h * SIDE:(h + 1) * SIDE]
        return carry

    lax.fori_loop(0, blocks, dense, 0)

    shares = [[], []]

    def arrived(h, ref):
        shares[h].append(mv.remote(ref, ref, twin))

    def gather_back(h):
        arrived(h, col_links.part(back[h], 0, 0))
        yield from gather_steps(mv, col_links, back[h], functools.partial(arrived, h))
        for share in shares[h]:
            yield
            share.wait_recv()

    gathers = [gather_back(h) for h in (0, 1)]
    advance(gathers[0], 1)
    for h in (0, 1):
        gt[h * SIDE:(h + 1) * SIDE, :] = lax.dot_general(
            hid[h][...].reshape(rows, SIDE), delta[...], (((0,), (0,)), ((), ())), preferred_element_type=F32
        )
    advance(gathers[0], 3)
    reduce = reduce_steps(mv, gt, wr1, wr2, wg_ref, row_peers, col_peers, nodes)
    while advance(gathers[0], 1):
        advance(gathers[1], 1)
    advance(reduce, 1)
    spread = [
        spread_steps(plan, 5, True, tiles, back[h], staged, panel[h], panel[h].shape[0], cuts)
        for h in (0, 1)
    ]
    for copy in forward_sends:
        copy.wait_send()
    while advance(spread[0], 1):
        advance(gathers[1], 1)
    scatters = [
        scatter_steps(mv, row_links, panel[h], b_bufs[h], fgt[h], lambda d, side: None) for h in (0, 1)
    ]
    advance(scatters[0], 9)
    while advance(gathers[1], 1):
        advance(scatters[0], 1)
    while advance(spread[1], 1):
        advance(scatters[0], 1)
    advance(scatters[1], 9)
    braid(scatters[0], scatters[1], reduce)

    def turn(i, carry):
        at = pl.ds(pl.multiple_of(i * SIDE, SIDE), SIDE)
        for h in (0, 1):
            fg_ref[at, h * SIDE:(h + 1) * SIDE] = fgt[h][i].T
        return carry

    lax.fori_loop(0, blocks, turn, 0)
    mv.drain()


def layer(plan, features, weight, cotangent, values, nodes):
    rows, width = features.shape
    total, size, _ = values.shape
    n_row, n_col = lax.axis_size("row"), lax.axis_size("col")
    any_spec = pl.BlockSpec(memory_space=pl.ANY)
    vmem = pl.BlockSpec(memory_space=pltpu.VMEM)
    blocks = rows // SIDE
    half = lambda count: [pltpu.VMEM((count * blocks, SIDE, SIDE), BF16)] * 2
    return pl.pallas_call(
        functools.partial(layer_kernel, nodes),
        out_shape=(
            jax.ShapeDtypeStruct((rows, width), BF16),
            jax.ShapeDtypeStruct((width, width), F32),
            jax.ShapeDtypeStruct((rows, width), BF16),
        ),
        in_specs=[pl.BlockSpec(memory_space=pltpu.SMEM), any_spec, vmem, any_spec, any_spec],
        out_specs=(vmem, vmem, vmem),
        scratch_shapes=[
            pltpu.VMEM((total, size, size), BF16),
            pltpu.VMEM((total, size, size), BF16),
            *half(n_row),
            *half(n_col),
            *half(n_col // 2),
            *half(n_col),
            *half(1),
            pltpu.VMEM((rows, width), BF16),
            pltpu.VMEM((rows, width), BF16),
            *half(1),
            pltpu.VMEM((width, width), F32),
            pltpu.VMEM((n_col, width // n_col, width), F32),
            pltpu.VMEM((n_row, width // n_col, width), F32),
            *(scatter_scratch(blocks) * 4),
            pltpu.SemaphoreType.DMA((280,)),
            pltpu.SemaphoreType.DMA((280,)),
            pltpu.SemaphoreType.DMA((4,)),
        ],
        compiler_params=pltpu.CompilerParams(
            collective_id=1, has_side_effects=True, vmem_limit_bytes=63 * 2**20
        ),
    )(plan, features.reshape(blocks, SIDE, width), weight, cotangent, values)


def sorted_slots(dest, anchor, count, blocks):
    total = dest.shape[0]
    slot = jnp.arange(total, dtype=jnp.int32)
    dest = jnp.where(slot < count, dest, blocks)
    key = dest * total + slot
    rank = jnp.sum((key[None, :] < key[:, None]).astype(jnp.int32), axis=1)
    here = rank[None, :] == slot[:, None]
    pick = lambda a: jnp.sum(jnp.where(here, a[None, :], 0), axis=1)
    ordered = pick(dest)
    before = jnp.sum((dest[None, :] < ordered[:, None]).astype(jnp.int32), axis=1)
    fresh = (before == slot).astype(jnp.int32)
    last = jnp.sum((dest[None, :] <= slot[:, None]).astype(jnp.int32), axis=1) - 1
    has = jnp.sum((dest[None, :] == slot[:, None]).astype(jnp.int32), axis=1)
    return [pick(slot), pick(anchor), fresh, jnp.maximum(last, 0), has]


def per_device(features, weight, cotangent, tile_values, tile_rows, tile_cols, tile_count):
    rows_idx = tile_rows[0, 0]
    cols_idx = tile_cols[0, 0]
    count = tile_count[0, 0]
    rows = features.shape[0]
    size = tile_values.shape[-1]
    n_row, n_col = lax.axis_size("row"), lax.axis_size("col")
    plan = jnp.stack(
        sorted_slots(rows_idx, cols_idx, count, rows * n_col // size)
        + sorted_slots(cols_idx, rows_idx, count, rows * n_row // size)
    )
    return layer(plan, features, weight, cotangent, tile_values[0, 0], rows * n_row * n_col)


def solution(mesh):
    return jax.shard_map(
        per_device,
        mesh=mesh,
        in_specs=(
            P(("col", "row"), None),
            P(),
            P(("row", "col"), None),
            P("row", "col", None, None, None),
            P("row", "col", None),
            P("row", "col", None),
            P("row", "col"),
        ),
        out_specs=(P(("row", "col"), None), P(), P(("col", "row"), None)),
        check_vma=False,
    )
```

time: 734 us -> 190 us (0.26)
  matrix products: 364 us -> 0 us
  waiting for transfers between devices: 282 us -> 0 us
  Pallas kernels: 0 us -> 178 us
  local copies, waits for them, and re-layouts: 57.2 us -> 6.67 us
  between operations: 13.8 us -> 1.36 us
  other arithmetic: 14.9 us -> 3.17 us
    dot_general x39 -> x0, matrix products: 364 us -> none  [the longest x12 237 us: step(): jnp.einsum('gt,gaf->taf', placer, prod, precision=lax.Precision.HIGHEST)]
    pallas_call x0 -> x1, Pallas kernels: none -> 178 us  [layer(): pl.pallas_call(functools.partial(layer_kernel, nodes), out_shape=(jax.Sha...]
    reduce_scatter x2 -> x0, waiting for transfers between devices: 157 us -> none  [the longest x1 84.1 us: per_device(): lax.psum_scatter(tpart, 'row', scatter_dimension=0, tiled=True)]
    all_gather x2 -> x0, waiting for transfers between devices: 125 us -> none  [the longest x1 75.1 us: per_device(): lax.all_gather(features, 'row', axis=0, tiled=True)]
    while x13 -> x0, local copies, waits for them, and re-layouts: 30.1 us -> none  [the longest x1 17 us: spread(): return lax.fori_loop(0, total // group, step, start_acc)]
    another operation x2 -> x7, local copies, waits for them, and re-layouts: 20.9 us -> 1.25 us  [per_device(): jnp.stack(sorted_slots(rows_idx, cols_idx, count, rows * n_col // size) +...]
    lt x12 -> x0, other arithmetic: 7.8 us -> none  [step(): live = start + jnp.arange(group, dtype=jnp.int32) < count]
  transfers between devices with their start and end apart: 5 -> 0, of which waited for: 4 -> 0; matrix products, arithmetic and copies ran while one was open for 29% -> 0% of each run, Pallas kernels for 0% -> 0%
where the time goes in v1:
time: 190 us; the launch traced here: 189 us
  Pallas kernels  178 us (94%)
  local copies, waits for them, and re-layouts  6.67 us (4%)
  other arithmetic  3.17 us (2%)
    pallas_call x1, Pallas kernels, layer(): pl.pallas_call(functools.partial(layer_kernel, nodes), out_shape=(jax.Sha...  178 us
    unnamed x3, local copies, waits for them, and re-layouts  5.4 us

profile of v1, /device:TPU:0, one launch (start us, length us, event | category | flops | bytes accessed | tf_op | source)
XLA Modules:
  0.0 189.4 jit_solution(3588637524505169230)
XLA Ops:
  1.3 0.7 reduce
  2.0 0.7 reduce.1
  2.7 0.2 convert_reduce_fusion.3
  2.9 0.2 convert_reduce_fusion.7
  3.2 0.3 select_reduce_fusion.3
  3.5 0.3 convert_reduce_fusion.4
  3.9 0.3 select_reduce_fusion
  4.2 0.3 convert_reduce_fusion
  4.5 1.2 stack.31.plan
  5.8 178.2 %shard_map.94 = (bf16[1024,256]{1,0:T(8,128)(2,1)}, f32[256,256]{1,0:T(8,128)}, bf16[1024,256]{1,0:T(8,128)(2,1)}) custom-call(s32[10,384]{1,0:T(8,128)} %stack.31.plan, bf16[8,128,256]{2,1,0:T(8,128)(2,1)} %bitcast.5, bf16[256,256]{1,0:T(8,128)(2,1)} %w_ref.1, bf16[1024,256]{1,0:T(8,128)(2,1)} %cot_ref.1, bf16[384,128,128]{2,1,0:T(8,128)(2,1)} %bitcast.4), custom_call_target="tpu_custom_call" | custom-call | tf_op jit(solution)/shard_map/pallas_call | solution.py:508
  184.0 1.9 copy.14
  185.9 1.7 copy.15
  187.6 1.9 copy.16
  (13 shorter events, 0.1 us)

commit v2 on v1

--- a/solution.py
+++ b/solution.py
@@ -9,7 +9,9 @@
 
 BF16 = jnp.bfloat16
 F32 = jnp.float32
-UNROLL = 24
+UNROLL = 32
+GATHER_SHARE = (2, 4)
+SCATTER_SHARE = (4, 2)
 SIDE = 128
 
 
@@ -72,18 +74,23 @@
 
 
 def add_blocks(dst, terms, blocks):
+    kind = BF16 if len(terms) == 2 else F32
+    group = 2 if blocks % 2 == 0 else 1
+
     def body(i, carry):
-        total = terms[0][i].astype(F32)
-        for term in terms[1:]:
-            total = total + term[i].astype(F32)
-        dst[i] = total.astype(dst.dtype)
+        for g in range(group):
+            at = i * group + g
+            total = terms[0][at].astype(kind)
+            for term in terms[1:]:
+                total = total + term[at].astype(kind)
+            dst[at] = total.astype(dst.dtype)
         return carry
 
-    lax.fori_loop(0, blocks, body, 0)
-
-
-def split(blocks):
-    first = blocks // 4
+    lax.fori_loop(0, blocks // group, body, 0)
+
+
+def split(blocks, share):
+    first = blocks // share
     rest = blocks - first
     return {
         "A": (0, first),
@@ -102,15 +109,15 @@
     def piece(self, d, side):
         return self.slot((self.p + d) % 4, self.q if side == 0 else 1 - self.q)
 
-    def part(self, ref, d, side, name=None):
-        start, size = split(self.blocks)[name] if name else (0, self.blocks)
+    def part(self, ref, d, side, name=None, share=2):
+        start, size = split(self.blocks, share)[name] if name else (0, self.blocks)
         return ref.at[pl.ds(self.piece(d, side) * self.blocks + start, size)]
 
 
-def gather_steps(mv, links, out, arrived):
+def gather_steps(mv, links, out, share, arrived):
     plus, minus = links.ring
     pair = links.pair
-    reg = functools.partial(links.part, out)
+    reg = functools.partial(links.part, out, share=share)
 
     def go(d, side, name, device):
         return mv.remote(reg(d, side, name), reg(d, side, name), device)
@@ -173,8 +180,8 @@
     arrived(reg(2, 1, "B"))
 
 
-def scatter_scratch(blocks):
-    parts = split(blocks)
+def scatter_scratch(blocks, share):
+    parts = split(blocks, share)
     first, rest = parts["A"][1], parts["B"][1]
     return [
         pltpu.VMEM((4, first, SIDE, SIDE), BF16),
@@ -189,13 +196,13 @@
 ORDER = ((2, 1), (2, 0), (1, 1), (3, 1), (1, 0), (3, 0), (0, 1), (0, 0))
 
 
-def scatter_steps(mv, links, held, bufs, out, ready):
-    parts = split(links.blocks)
+def scatter_steps(mv, links, held, share, bufs, out, ready):
+    parts = split(links.blocks, share)
     plus, minus = links.ring
     pair = links.pair
     ra, rb1, rb2, ra1, ra2, rp = bufs
     nb, na = parts["B"][1], parts["A"][1]
-    reg = functools.partial(links.part, held)
+    reg = functools.partial(links.part, held, share=share)
     b_half = lambda ref, h: ref.at[pl.ds(h * (nb // 2), nb // 2)]
     a_half = lambda ref, h: ref.at[pl.ds(h * (na // 2), na // 2)]
     got_b1, got_b2, got_a, got_a2 = {}, {}, {}, {}
@@ -260,25 +267,33 @@
     add_blocks(out.at[pl.ds(0, na)], [reg(0, 0, "A"), ra.at[0], ra2.at[0], ra2.at[1]], na)
 
 
-def spread_steps(plan, base, flip, tiles, source, staged, out, blocks, cuts):
-    total = tiles.shape[0]
-    perm, anchor, fresh, last, has = (functools.partial(lambda row, i: plan[row, i], base + j) for j in range(5))
+def spread_steps(plan, which, flip, tiles, source, staged, out, cuts):
+    read = lambda row: lambda i: plan[which, row, i]
+    tile0, tile1, anchor0, anchor1, fresh, last, has = (read(row) for row in range(7))
 
     def body(i, acc):
         first = i * UNROLL
         prods = []
         for u in range(UNROLL):
-            tile = tiles[perm(first + u)]
-            other = source[anchor(first + u)]
-            left, right = (other, tile) if flip else (tile, other)
-            prods.append(jnp.dot(left, right, preferred_element_type=F32))
+            at = first + u
+            pair = (tiles[tile0(at)], tiles[tile1(at)])
+            other = (source[anchor0(at)], source[anchor1(at)])
+            left, right = (other, pair) if flip else (pair, other)
+            prods.append(
+                jnp.dot(
+                    jnp.concatenate(left, axis=1),
+                    jnp.concatenate(right, axis=0),
+                    preferred_element_type=F32,
+                )
+            )
         for u in range(UNROLL):
             begins = jnp.full((SIDE, SIDE), fresh(first + u), jnp.int32) != 0
             acc = jnp.where(begins, 0.0, acc) + prods[u]
             staged[first + u] = acc.astype(BF16)
         return acc
 
-    steps = total // UNROLL
+    blocks = out.shape[0]
+    steps = pair_slots(tiles.shape[0] - 1, blocks) // UNROLL
     acc = jnp.zeros((SIDE, SIDE), F32)
     for cut in range(cuts):
         acc = lax.fori_loop(cut * steps // cuts, (cut + 1) * steps // cuts, body, acc)
@@ -297,38 +312,31 @@
     lax.fori_loop(0, blocks // group, put, 0)
 
 
-def reduce_steps(mv, gt, wr1, wr2, wg_ref, row_peers, col_peers, nodes):
-    r0 = lax.axis_index("row")
-    c0 = lax.axis_index("col")
-    n_row, n_col = len(row_peers) + 1, len(col_peers) + 1
-    depth = gt.shape[0] // n_col
-
-    def strip(c):
-        return pl.ds(pl.multiple_of(c * depth, depth), depth)
-
-    first = [
-        mv.remote(gt.at[strip((c0 + j) % n_col)], wr1.at[j], col_peers[j - 1])
-        for j in range(1, n_col)
-    ]
-    yield
-    for copy in first:
+def reduce_steps(mv, gt, met_rows, met_strips, strips, wg_ref, halvings, doublings, nodes):
+    start, size = 0, gt.shape[0]
+    rows = lambda start, size: pl.ds(pl.multiple_of(start, 8), size)
+    for i, (device, bit) in enumerate(halvings):
+        size //= 2
+        land = met_rows.at[pl.ds(size, size)]
+        copy = mv.remote(gt.at[rows(start + (1 - bit) * size, size)], land, device)
+        start = start + bit * size
+        yield
         copy.wait_recv()
-    total = gt[strip(c0), :]
-    for j in range(1, n_col):
-        total = total + wr1[j]
-    wr2[r0] = total
-    second = [mv.remote(wr2.at[r0], wr2.at[r0], peer) for peer in row_peers]
-    yield
-    for copy in second:
+        keep = rows(start, size)
+        gt[keep, :] = gt[keep, :] + land[...]
+    strips[0] = gt[rows(start, size), :]
+    for i, device in enumerate(doublings):
+        copy = mv.remote(strips.at[i], met_strips.at[i], device)
+        yield
         copy.wait_recv()
-    total = wr2[0]
-    for j in range(1, n_row):
-        total = total + wr2[j]
-    wg_ref[strip(c0), :] = total / jnp.sqrt(F32(nodes))
-    third = [mv.remote(wg_ref.at[strip(c0)], wg_ref.at[strip(c0)], peer) for peer in col_peers]
-    yield
-    for copy in third:
+        strips[i + 1] = strips[i] + met_strips[i]
+    wg_ref[rows(start, size), :] = strips[len(doublings)] / jnp.sqrt(F32(nodes))
+    for device, bit in reversed(halvings):
+        copy = mv.remote(wg_ref.at[rows(start, size)], wg_ref.at[rows(start, size)], device)
+        yield
         copy.wait_recv()
+        start = start - bit * size
+        size *= 2
 
 
 def advance(steps, count=None):
@@ -348,10 +356,40 @@
         left = [s for s in left if advance(s, 1)]
 
 
+def both(main, other):
+    for step in main:
+        advance(other, 1)
+        yield step
+
+
+def weave(gather, scatter, spread):
+    advance(scatter, 1)
+    advance(gather, 1)
+    advance(scatter, 2)
+    advance(gather, 1)
+    advance(scatter, 4)
+    advance(gather, 1)
+    advance(scatter, 2)
+    advance(gather, 2)
+    advance(scatter, 1)
+    advance(gather)
+    while advance(spread, 1):
+        advance(scatter, 1)
+
+
+def weave_ends(early, late, sends):
+    advance(late, 5)
+    advance(early, 1)
+    advance(late, 4)
+    for copy in sends:
+        copy.wait_send()
+    braid(early, late)
+
+
 def layer_kernel(
-    nodes, plan, x_ref, w_ref, cot_ref, tiles_ref, act_ref, wg_ref, fg_ref,
+    nodes, plan, x_ref, w_ref, cot_ref, tiles_ref, act_ref, wg_ref, fgt0, fgt1,
     tiles, staged, panel0, panel1, part0, part1, met0, met1, back0, back1,
-    hid0, hid1, delta, cot, fgt0, fgt1, gt, wr1, wr2, *rest
+    hid0, hid1, delta, cot, gt, met_rows, met_strips, strips, *rest
 ):
     f_bufs = (rest[0:6], rest[6:12])
     b_bufs = (rest[12:18], rest[18:24])
@@ -359,10 +397,8 @@
     panel, part, met, back = (panel0, panel1), (part0, part1), (met0, met1), (back0, back1)
     hid, fgt = (hid0, hid1), (fgt0, fgt1)
     z, xh, xl, y, k = place()
-    r0, c0 = lax.axis_index("row"), lax.axis_index("col")
     rows = cot.shape[0]
     blocks = rows // SIDE
-    n_row, n_col = lax.axis_size("row"), lax.axis_size("col")
 
     row_slot = lambda p, q: p * 2 + q
     col_slot = lambda p, q: (q * 4 + p) * 2 + k
@@ -377,52 +413,57 @@
     loads = [
         mv.local(x_ref.at[:, :, pl.ds(h * SIDE, SIDE)], row_links.part(panel[h], 0, 0)) for h in (0, 1)
     ]
-    load_tiles = mv.local(tiles_ref, tiles)
+    count = tiles_ref.shape[0]
+    load_tiles = mv.local(tiles_ref, tiles.at[pl.ds(0, count)])
+    tiles[count] = jnp.zeros((SIDE, SIDE), BF16)
     load_cot = mv.local(cot_ref, cot)
-    row_peers = [((r0 + j) % n_row, c0) for j in range(1, n_row)]
-    col_peers = [(r0, (c0 + j) % n_col) for j in range(1, n_col)]
-    greet(row_peers + col_peers)
-
-    gathers = [gather_steps(mv, row_links, panel[h], lambda ref: None) for h in (0, 1)]
+    greet([*row_links.ring, row_links.pair, *col_links.ring, col_links.pair, twin])
+
+    gathers = [gather_steps(mv, row_links, panel[h], GATHER_SHARE[h], lambda ref: None) for h in (0, 1)]
     loads[0].wait()
-    advance(gathers[0], 4)
+    advance(gathers[0], 7)
     loads[1].wait()
-    while advance(gathers[0], 1):
-        advance(gathers[1], 1)
+    advance(gathers[1], 1)
+    advance(gathers[0])
     load_tiles.wait()
 
     def twin_steps(h):
         crossing = {}
-        for d, side in ORDER:
-            piece = (y + d) % 4 + 4 * (xl if side == 0 else 1 - xl)
-            from_part = part[h].at[pl.ds((piece * 2 + 1 - k) * blocks, blocks)]
-            to_met = met[h].at[pl.ds(piece * blocks, blocks)]
-            crossing[d, side] = (mv.remote(from_part, to_met, twin), to_met)
+        to_cross = list(ORDER)
+
+        def cross(count):
+            for d, side in to_cross[:count]:
+                piece = (y + d) % 4 + 4 * (xl if side == 0 else 1 - xl)
+                from_part = part[h].at[pl.ds((piece * 2 + 1 - k) * blocks, blocks)]
+                to_met = met[h].at[pl.ds(piece * blocks, blocks)]
+                crossing[d, side] = (mv.remote(from_part, to_met, twin), to_met)
+            del to_cross[:count]
+
+        cross(3)
 
         def ready(d, side):
+            cross(1)
             copy, land = crossing[d, side]
             copy.wait_recv()
             ref = col_links.part(part[h], d, side)
             add_blocks(ref, [ref, land], blocks)
 
-        yield from scatter_steps(mv, col_links, part[h], f_bufs[h], hid[h], ready)
-
-    cuts = 8
+        yield from scatter_steps(mv, col_links, part[h], SCATTER_SHARE[h], f_bufs[h], hid[h], ready)
+
+    cuts = 4
     spread = [
-        spread_steps(plan, 0, False, tiles, panel[h], staged, part[h], part[h].shape[0], cuts)
+        spread_steps(plan, 0, False, tiles, panel[h], staged, part[h], cuts)
         for h in (0, 1)
     ]
-    while advance(spread[0], 1):
-        advance(gathers[1], 1)
+    advance(spread[0], 2)
+    advance(gathers[1], 1)
+    advance(spread[0], 1)
+    advance(gathers[1], 1)
+    advance(spread[0])
     scatters = [twin_steps(h) for h in (0, 1)]
-    advance(scatters[0], 4)
-    while advance(gathers[1], 1):
-        advance(scatters[0], 1)
-    while advance(spread[1], 1):
-        advance(scatters[0], 1)
+    weave(gathers[1], scatters[0], spread[1])
     forward_sends = mv.take()
-    advance(scatters[1], 8)
-    braid(scatters[0], scatters[1])
+    weave_ends(scatters[0], scatters[1], [])
 
     load_cot.wait()
     weight = w_ref[...]
@@ -452,9 +493,9 @@
 
     def gather_back(h):
         arrived(h, col_links.part(back[h], 0, 0))
-        yield from gather_steps(mv, col_links, back[h], functools.partial(arrived, h))
+        yield from gather_steps(mv, col_links, back[h], GATHER_SHARE[h], functools.partial(arrived, h))
+        yield
         for share in shares[h]:
-            yield
             share.wait_recv()
 
     gathers = [gather_back(h) for h in (0, 1)]
@@ -463,37 +504,39 @@
         gt[h * SIDE:(h + 1) * SIDE, :] = lax.dot_general(
             hid[h][...].reshape(rows, SIDE), delta[...], (((0,), (0,)), ((), ())), preferred_element_type=F32
         )
-    advance(gathers[0], 3)
-    reduce = reduce_steps(mv, gt, wr1, wr2, wg_ref, row_peers, col_peers, nodes)
-    while advance(gathers[0], 1):
-        advance(gathers[1], 1)
-    advance(reduce, 1)
-    spread = [
-        spread_steps(plan, 5, True, tiles, back[h], staged, panel[h], panel[h].shape[0], cuts)
-        for h in (0, 1)
-    ]
     for copy in forward_sends:
         copy.wait_send()
-    while advance(spread[0], 1):
-        advance(gathers[1], 1)
+    advance(gathers[0], 6)
+    near = lambda i: i + 1 - 2 * (i % 2)
+    halvings = (
+        (twin, k),
+        (col_links.pair, xl),
+        (col_device(xl, near(y), k), (y + 1) // 2 % 2),
+        (col_device(xl, 3 - y, k), y // 2),
+    )
+    doublings = (row_links.pair, row_device(near(z), xh), row_device(3 - z, xh))
+    reduce = reduce_steps(mv, gt, met_rows, met_strips, strips, wg_ref, halvings, doublings, nodes)
+    advance(reduce, 1)
+    advance(gathers[1], 1)
+    advance(gathers[0])
+    spread = [
+        spread_steps(plan, 1, True, tiles, back[h], staged, panel[h], cuts) for h in (0, 1)
+    ]
+    advance(spread[0], 2)
+    advance(gathers[1], 1)
+    advance(reduce, 1)
+    advance(spread[0], 1)
+    advance(gathers[1], 1)
+    advance(reduce, 1)
+    advance(spread[0])
     scatters = [
-        scatter_steps(mv, row_links, panel[h], b_bufs[h], fgt[h], lambda d, side: None) for h in (0, 1)
+        scatter_steps(mv, row_links, panel[h], SCATTER_SHARE[h], b_bufs[h], fgt[h], lambda d, side: None) for h in (0, 1)
     ]
-    advance(scatters[0], 9)
-    while advance(gathers[1], 1):
-        advance(scatters[0], 1)
-    while advance(spread[1], 1):
-        advance(scatters[0], 1)
-    advance(scatters[1], 9)
-    braid(scatters[0], scatters[1], reduce)
-
-    def turn(i, carry):
-        at = pl.ds(pl.multiple_of(i * SIDE, SIDE), SIDE)
-        for h in (0, 1):
-            fg_ref[at, h * SIDE:(h + 1) * SIDE] = fgt[h][i].T
-        return carry
-
-    lax.fori_loop(0, blocks, turn, 0)
+    weave(gathers[1], scatters[0], both(spread[1], reduce))
+    backward_sends = mv.take()
+    weave_ends(scatters[0], both(scatters[1], reduce), backward_sends)
+    advance(reduce)
+
     mv.drain()
 
 
@@ -510,13 +553,13 @@
         out_shape=(
             jax.ShapeDtypeStruct((rows, width), BF16),
             jax.ShapeDtypeStruct((width, width), F32),
-            jax.ShapeDtypeStruct((rows, width), BF16),
+            *[jax.ShapeDtypeStruct((blocks, SIDE, SIDE), BF16)] * 2,
         ),
         in_specs=[pl.BlockSpec(memory_space=pltpu.SMEM), any_spec, vmem, any_spec, any_spec],
-        out_specs=(vmem, vmem, vmem),
+        out_specs=(vmem,) * 4,
         scratch_shapes=[
-            pltpu.VMEM((total, size, size), BF16),
-            pltpu.VMEM((total, size, size), BF16),
+            pltpu.VMEM((total + 1, size, size), BF16),
+            pltpu.VMEM((pair_slots(total, n_col * blocks), size, size), BF16),
             *half(n_row),
             *half(n_col),
             *half(n_col // 2),
@@ -524,11 +567,11 @@
             *half(1),
             pltpu.VMEM((rows, width), BF16),
             pltpu.VMEM((rows, width), BF16),
-            *half(1),
             pltpu.VMEM((width, width), F32),
-            pltpu.VMEM((n_col, width // n_col, width), F32),
-            pltpu.VMEM((n_row, width // n_col, width), F32),
-            *(scatter_scratch(blocks) * 4),
+            pltpu.VMEM((width, width), F32),
+            pltpu.VMEM((3, width // n_col, width), F32),
+            pltpu.VMEM((4, width // n_col, width), F32),
+            *((scatter_scratch(blocks, SCATTER_SHARE[0]) + scatter_scratch(blocks, SCATTER_SHARE[1])) * 2),
             pltpu.SemaphoreType.DMA((280,)),
             pltpu.SemaphoreType.DMA((280,)),
             pltpu.SemaphoreType.DMA((4,)),
@@ -539,20 +582,56 @@
     )(plan, features.reshape(blocks, SIDE, width), weight, cotangent, values)
 
 
-def sorted_slots(dest, anchor, count, blocks):
+def unfold_kernel(act_ref, wg_ref, fgt0, fgt1, act_out, wg_out, fg_out):
+    def body(i, carry):
+        at = pl.ds(pl.multiple_of(i * SIDE, SIDE), SIDE)
+        act_out[at, :] = act_ref[at, :]
+        fg_out[at, :] = jnp.concatenate([fgt0[i].T, fgt1[i].T], axis=1)
+        return carry
+
+    lax.fori_loop(0, fgt0.shape[0], body, 0)
+    wg_out[...] = wg_ref[...]
+
+
+def unfold(activated, weight_grad, turned0, turned1):
+    vmem = pl.BlockSpec(memory_space=pltpu.VMEM)
+    like = lambda a: jax.ShapeDtypeStruct(a.shape, a.dtype)
+    return pl.pallas_call(
+        unfold_kernel,
+        out_shape=(like(activated), like(weight_grad), like(activated)),
+        in_specs=[vmem] * 4,
+        out_specs=(vmem,) * 3,
+    )(activated, weight_grad, turned0, turned1)
+
+
+def pair_slots(total, blocks):
+    need = (total + blocks) // 2
+    return -(-need // UNROLL) * UNROLL
+
+
+def paired_slots(dest, anchor, count, blocks, room):
     total = dest.shape[0]
     slot = jnp.arange(total, dtype=jnp.int32)
-    dest = jnp.where(slot < count, dest, blocks)
-    key = dest * total + slot
-    rank = jnp.sum((key[None, :] < key[:, None]).astype(jnp.int32), axis=1)
-    here = rank[None, :] == slot[:, None]
-    pick = lambda a: jnp.sum(jnp.where(here, a[None, :], 0), axis=1)
-    ordered = pick(dest)
-    before = jnp.sum((dest[None, :] < ordered[:, None]).astype(jnp.int32), axis=1)
-    fresh = (before == slot).astype(jnp.int32)
-    last = jnp.sum((dest[None, :] <= slot[:, None]).astype(jnp.int32), axis=1) - 1
-    has = jnp.sum((dest[None, :] == slot[:, None]).astype(jnp.int32), axis=1)
-    return [pick(slot), pick(anchor), fresh, jnp.maximum(last, 0), has]
+    block = jnp.arange(room, dtype=jnp.int32)
+    add = lambda hit, value=1: jnp.sum(jnp.where(hit, value, 0), axis=1, dtype=jnp.int32)
+    live = slot < count
+    dest = jnp.where(live, dest, blocks)
+    mine = add(dest[None, :] == block[:, None])
+    pairs = (mine + 1) // 2
+    start = add(block[None, :] < block[:, None], pairs[None, :])
+    order = add((dest[None, :] == dest[:, None]) & (slot[None, :] < slot[:, None]))
+    begin = add(dest[:, None] == block[None, :], start[None, :])
+    at = jnp.where(live, begin + order // 2, room)
+    here = at[None, :] == block[:, None]
+    first = here & (order % 2 == 0)[None, :]
+    second = here & (order % 2 == 1)[None, :]
+    alone = 1 - add(second)
+    tile0 = add(first, slot[None, :])
+    tile1 = add(second, slot[None, :]) + alone * total
+    anchor0 = add(first, anchor[None, :])
+    anchor1 = add(second, anchor[None, :]) + alone * anchor0
+    fresh = add(first & (order == 0)[None, :])
+    return jnp.stack([tile0, tile1, anchor0, anchor1, fresh, jnp.maximum(start + pairs - 1, 0), mine])
 
 
 def per_device(features, weight, cotangent, tile_values, tile_rows, tile_cols, tile_count):
@@ -562,11 +641,16 @@
     rows = features.shape[0]
     size = tile_values.shape[-1]
     n_row, n_col = lax.axis_size("row"), lax.axis_size("col")
-    plan = jnp.stack(
-        sorted_slots(rows_idx, cols_idx, count, rows * n_col // size)
-        + sorted_slots(cols_idx, rows_idx, count, rows * n_row // size)
+    row_blocks, col_blocks = rows * n_col // size, rows * n_row // size
+    room = pair_slots(rows_idx.shape[0], row_blocks)
+    plan = jax.vmap(paired_slots, in_axes=(0, 0, None, 0, None))(
+        jnp.stack([rows_idx, cols_idx]),
+        jnp.stack([cols_idx, rows_idx]),
+        count,
+        jnp.array([row_blocks, col_blocks], jnp.int32),
+        room,
     )
-    return layer(plan, features, weight, cotangent, tile_values[0, 0], rows * n_row * n_col)
+    return unfold(*layer(plan, features, weight, cotangent, tile_values[0, 0], rows * n_row * n_col))
 
 
 def solution(mesh):

time: 190 us -> 165 us (0.87)
  Pallas kernels: 178 us -> 160 us
  local copies, waits for them, and re-layouts: 6.67 us -> 0.65 us
    pallas_call x1, Pallas kernels: 178 us -> 157 us  [layer(): pl.pallas_call(functools.partial(layer_kernel, nodes), out_shape=(jax.Sha...]
    unnamed x3 -> x0, local copies, waits for them, and re-layouts: 5.4 us -> none
    pallas_call x0 -> x1, Pallas kernels: none -> 2.85 us  [unfold(): pl.pallas_call(unfold_kernel, out_shape=(like(activated), like(weight_gra...]
where the time goes in v2:
time: 165 us
  Pallas kernels  160 us (97%)
  other arithmetic  3.02 us (2%)
    pallas_call x1, Pallas kernels, layer(): pl.pallas_call(functools.partial(layer_kernel, nodes), out_shape=(jax.Sha...  157 us

profile of v2, /device:TPU:0, one launch (start us, length us, event | category | flops | bytes accessed | tf_op | source)
XLA Modules:
  0.0 164.6 jit_solution(8604594265806193823)
XLA Ops:
  1.3 0.8 add_select_fusion
  2.1 0.2 select_reduce_fusion.8
  2.3 0.2 select_reduce_fusion.9
  2.5 0.3 select_reduce_fusion.7
  2.9 0.5 select_reduce_fusion
  3.4 0.9 select_reduce_fusion.2
  4.4 0.6 stack.33
  5.0 156.7 %shard_map.103 = (bf16[1024,256]{1,0:T(8,128)(2,1)}, f32[256,256]{1,0:T(8,128)}, bf16[8,128,128]{2,1,0:T(8,128)(2,1)}, bf16[8,128,128]{2,1,0:T(8,128)(2,1)}) custom-call(s32[2,7,256]{2,1,0:T(8,128)} %bitcast.9, bf16[8,128,256]{2,1,0:T(8,128)(2,1)} %bitcast.8, bf16[256,256]{1,0:T(8,128)(2,1)} %w_ref.1, bf16[1024,256]{1,0:T(8,128)(2,1)} %cot_ref.1, ...), custom_call_target="tpu_custom_call" | custom-call | tf_op jit(solution)/shard_map/pallas_call | solution.py:551
  161.8 2.8 %shard_map.104 = (bf16[1024,256]{1,0:T(8,128)(2,1)}, f32[256,256]{1,0:T(8,128)}, bf16[1024,256]{1,0:T(8,128)(2,1)}) custom-call(bf16[1024,256]{1,0:T(8,128)(2,1)} %get-tuple-element.7.act_ref, f32[256,256]{1,0:T(8,128)} %get-tuple-element.8.wg_ref, bf16[8,128,128]{2,1,0:T(8,128)(2,1)} %get-tuple-element.9.fgt0, bf16[8,128,128]{2,1,0:T(8,128)(2,1)} %get-tuple-element.10.fgt1), custom_call_target="tpu_custom_call" | custom-call | tf_op jit(solution)/shard_map/pallas_call | solution.py:599
  (13 shorter events, 0.2 us)

commit v3 on v2

--- a/solution.py
+++ b/solution.py
@@ -365,14 +365,11 @@
 def weave(gather, scatter, spread):
     advance(scatter, 1)
     advance(gather, 1)
-    advance(scatter, 2)
-    advance(gather, 1)
-    advance(scatter, 4)
-    advance(gather, 1)
-    advance(scatter, 2)
-    advance(gather, 2)
+    advance(scatter, 8)
+    advance(gather, 4)
     advance(scatter, 1)
     advance(gather)
+    advance(scatter, 1)
     while advance(spread, 1):
         advance(scatter, 1)
 

time: 165 us -> 158 us (0.958)
  Pallas kernels: 160 us -> 151 us
    pallas_call x1, Pallas kernels: 157 us -> 149 us  [layer(): pl.pallas_call(functools.partial(layer_kernel, nodes), out_shape=(jax.Sha...]
where the time goes in v3:
time: 158 us; the launch traced here: 156 us
  Pallas kernels  151 us (96%)
  other arithmetic  3.02 us (2%)
    pallas_call x1, Pallas kernels, layer(): pl.pallas_call(functools.partial(layer_kernel, nodes), out_shape=(jax.Sha...  149 us

profile of v3, /device:TPU:0, one launch (start us, length us, event | category | flops | bytes accessed | tf_op | source)
XLA Modules:
  0.0 156.5 jit_solution(1839036345238651569)
XLA Ops:
  1.3 0.8 add_select_fusion
  2.1 0.2 select_reduce_fusion.8
  2.3 0.2 select_reduce_fusion.9
  2.5 0.3 select_reduce_fusion.7
  2.9 0.5 select_reduce_fusion
  3.4 0.9 select_reduce_fusion.2
  4.4 0.6 stack.33
  5.0 148.6 %shard_map.103 = (bf16[1024,256]{1,0:T(8,128)(2,1)}, f32[256,256]{1,0:T(8,128)}, bf16[8,128,128]{2,1,0:T(8,128)(2,1)}, bf16[8,128,128]{2,1,0:T(8,128)(2,1)}) custom-call(s32[2,7,256]{2,1,0:T(8,128)} %bitcast.9, bf16[8,128,256]{2,1,0:T(8,128)(2,1)} %bitcast.8, bf16[256,256]{1,0:T(8,128)(2,1)} %w_ref.1, bf16[1024,256]{1,0:T(8,128)(2,1)} %cot_ref.1, ...), custom_call_target="tpu_custom_call" | custom-call | tf_op jit(solution)/shard_map/pallas_call | solution.py:548
  153.6 2.8 %shard_map.104 = (bf16[1024,256]{1,0:T(8,128)(2,1)}, f32[256,256]{1,0:T(8,128)}, bf16[1024,256]{1,0:T(8,128)(2,1)}) custom-call(bf16[1024,256]{1,0:T(8,128)(2,1)} %get-tuple-element.7.act_ref, f32[256,256]{1,0:T(8,128)} %get-tuple-element.8.wg_ref, bf16[8,128,128]{2,1,0:T(8,128)(2,1)} %get-tuple-element.9.fgt0, bf16[8,128,128]{2,1,0:T(8,128)(2,1)} %get-tuple-element.10.fgt1), custom_call_target="tpu_custom_call" | custom-call | tf_op jit(solution)/shard_map/pallas_call | solution.py:596
  (13 shorter events, 0.2 us)
